TPU v7x, 32 devices: a whole 2x2x4 slice. The times are simulated.
32 devices in a mesh: grp: 4 (over x, core), dev: 8 (over z, y).
Axes of the slice: x: 2, y: 2, z: 4, core: 2. Of those that a mesh axis runs over, the one named last changes fastest.
Arguments:
- traces: float32 [32, 16, 128], P(('grp', 'dev')), parts along dimension 0
- half_window: int32 [32], P(('grp', 'dev')), parts along dimension 0, may hold values from 4 to 23
- dip_slopes: int32 [9], replicated, may hold values from -4 to 4, as said below
Outputs:
- coherence: float32 [32, 16, 128], P('grp', 'dev'), parts along dimension 0
There are 4 independent parts, one for each index of `grp`. A program takes and returns all parts, laid end to end along the dimension named above; an argument that names none is the same for every part. Nothing has to cross between parts.
Inputs may be any that keep to these rules, and one draw needn't show every extreme that they name: `dip_slopes`: each trial dip is a whole number of samples per shot; both extreme dips occur.
All inputs are finite; a program needn't handle non-finite values.
Results may differ from a plain program's by a relative error of at most 0.00005.
Values sent between devices are 32-bit elements; how exact they have to be, the bound alone decides.
A program may use at most 64 MiB of HBM per device.

v0:
```python
import jax
import jax.numpy as jnp
from jax import lax
from jax.sharding import PartitionSpec as P

floor_level = 0.05


def extended_2(value, sides, width):
    for axis, dim in sides:
        size, length = (lax.axis_size(axis), value.shape[dim])
        up = [(i, (i + 1) % size) for i in range(size - 1)]
        down = [(j, i) for i, j in up]
        last = lax.slice_in_dim(value, length - width, length, axis=dim)
        initial = lax.slice_in_dim(value, 0, width, axis=dim)
        before = lax.ppermute(last, axis, up)
        after = lax.ppermute(initial, axis, down)
        value = jnp.concatenate([before, value, after], axis=dim)
    return value


def gain_control(traces, half_window):
    samples = jnp.arange(traces.shape[-1], dtype=jnp.int32)
    distance = jnp.abs(samples[:, None] - samples[None, :])
    window_mask = (distance[None, :, :] <= half_window[:, None, None]).astype(jnp.float32)
    window_count = jnp.sum(window_mask, axis=1)
    power_sum = jnp.einsum(
        "srt,stu->sru", traces * traces, window_mask, precision=lax.Precision.HIGHEST
    )
    mean_square = power_sum / window_count[:, None, :]
    return traces * lax.rsqrt(jnp.maximum(mean_square, floor_level))


def semblance_scan(widened, dip_slopes):
    shot_count = widened.shape[0]
    wide = widened.shape[1]
    length = widened.shape[2]
    inner = wide - 4
    padded = jnp.pad(widened, ((2, 2), (0, 0), (13, 13)))
    extended = length + 10
    later = jnp.arange(extended, dtype=jnp.int32)[:, None]
    earlier = jnp.arange(length, dtype=jnp.int32)[None, :]
    lag_gap = later - earlier
    time_band = ((lag_gap >= 0) & (lag_gap <= 10)).astype(jnp.float32)
    coherent = None
    for which in range(dip_slopes.shape[0]):
        slope = dip_slopes[which]
        stacked = jnp.zeros((shot_count, wide, extended), jnp.float32)
        energy_sum = jnp.zeros((shot_count, wide, extended), jnp.float32)
        for member in range(5):
            offset = member - 2
            rows = padded[member : member + shot_count, :, :]
            start = 8 + offset * slope
            shifted = lax.dynamic_slice_in_dim(rows, start, extended, 2)
            stacked = stacked + shifted
            energy_sum = energy_sum + shifted * shifted
        squared = stacked * stacked
        squared_rows = squared[:, 0:inner, :]
        energy_rows = energy_sum[:, 0:inner, :]
        for across in range(1, 5):
            squared_rows = squared_rows + squared[:, across : across + inner, :]
            energy_rows = energy_rows + energy_sum[:, across : across + inner, :]
        numerator = jnp.dot(
            squared_rows.reshape(shot_count * inner, extended),
            time_band,
            precision=lax.Precision.HIGHEST,
            preferred_element_type=jnp.float32,
        )
        denominator = jnp.dot(
            energy_rows.reshape(shot_count * inner, extended),
            time_band,
            precision=lax.Precision.HIGHEST,
            preferred_element_type=jnp.float32,
        )
        current = (numerator / (5.0 * denominator + 1.0)).reshape(shot_count, inner, length)
        coherent = current if coherent is None else jnp.maximum(coherent, current)
    return coherent


def body(traces, half_window, dip_slopes):
    balanced = gain_control(traces, half_window)
    gathered = lax.all_to_all(balanced, "dev", split_axis=1, concat_axis=0, tiled=True)
    widened = extended_2(gathered, (("dev", 1),), 2)
    return semblance_scan(widened, dip_slopes)


def solution(mesh):
    return jax.shard_map(
        body,
        mesh=mesh,
        in_specs=(P(("grp", "dev"), None, None), P(("grp", "dev")), P()),
        out_specs=P("grp", "dev", None),
        check_vma=False,
    )
```

profile of v0, /device:TPU:0, one launch (start us, length us, event | category | flops | bytes accessed | tf_op | source)
XLA Modules:
  0.0 51.2 jit_solution(14853539897846402921)
XLA Ops:
  0.7 1.5 %fusion.29 = f32[1,16,128]{2,1,0:T(8,128)} fusion(f32[1,16,128]{2,1,0:T(8,128)} %param.3, s32[]{:T(128)} %bitcast.104, f32[128]{0:T(128)S(1)} %convert_reduce_fusion), kind=kOutput, calls=%fused_computation.39 | convolution fusion | flops 3203072 | bytes 16900 | tf_op jit(solution)/shard_map/srt,stu->sru/dot_general | solution.py:27
  2.2 7.4 %all-to-all-start = ((f32[1,16,128]{2,0,1:T(1,128)}), f32[1,16,128]{2,0,1:T(1,128)S(1)}, u32[]{:S(2)}, u32[]{:S(2)}) async-start(f32[1,16,128]{2,0,1:T(1,128)} %bitcast.4), calls=%async_computation | async-start | bytes 16384 | tf_op jit(solution)/shard_map/all_to_all | solution.py:82
  9.7 0.7 %fusion.105 = (s32[1]{0:T(128)}, s32[1]{0:T(128)}, s32[1]{0:T(128)}, s32[1]{0:T(128)}, s32[1]{0:T(128)}, /*index=5*/s32[1]{0:T(128)}, s32[1]{0:T(128)}, s32[1]{0:T(128)}, s32[1]{0:T(128)}) fusion(s32[9]{0:T(128)S(1)} %copy-done), kind=kLoop, calls=%fused_computation.196 | loop fusion | bytes 72 | tf_op jit(solution)/shard_map/slice | solution.py:47
  32.6 1.3 %collective-permute-start.1 = (f32[8,2,128]{2,1,0:T(2,128)S(1)}, f32[8,2,128]{2,1,0:T(2,128)S(1)}, u32[]{:S(2)}, u32[]{:S(2)}) collective-permute-start(f32[8,2,128]{2,1,0:T(2,128)S(1)} %bitcast.106), channel_id=1, source_target_pairs={{1,0},{2,1},{3,2},{4,3},{5,4},{6,5},{7,6},{9,8},{10,9},{11,10},{12... | collective-permute-start | bytes 24584 | tf_op jit(solution)/shard_map/ppermute | solution.py:17
  33.9 4.5 %collective-permute-start = (f32[8,2,128]{2,1,0:T(2,128)S(1)}, f32[8,2,128]{2,1,0:T(2,128)S(1)}, u32[]{:S(2)}, u32[]{:S(2)}) collective-permute-start(f32[8,2,128]{2,1,0:T(2,128)S(1)} %bitcast.107), channel_id=1, source_target_pairs={{0,1},{1,2},{2,3},{3,4},{4,5},{5,6},{6,7},{8,9},{9,10},{10,11},{11... | collective-permute-start | bytes 24584 | tf_op jit(solution)/shard_map/ppermute | solution.py:16
  44.6 0.1 select_maximum_fusion
  44.7 0.3 add_multiply_fusion.6
  45.1 0.1 fusion.63
  45.2 0.3 multiply_add_fusion
  45.7 0.1 fusion.60
  45.9 0.1 slice_add_fusion
  46.0 0.1 fusion.57
  46.1 0.3 add_multiply_fusion
  46.5 0.3 add_multiply_fusion.3
  46.9 0.1 fusion.54
  47.1 0.1 slice_add_fusion.4
  47.3 0.1 fusion.51
  47.4 0.3 multiply_add_fusion.1
  47.8 0.1 fusion.48
  48.1 0.2 add_multiply_fusion.1
  48.4 0.1 fusion.45
  48.6 0.1 fusion.42
  48.8 0.1 fusion.39
  49.0 0.1 fusion.25
  49.2 0.2 fusion.23
  49.4 0.2 fusion.20
  49.5 0.2 fusion.17
  49.7 0.2 fusion.14
  49.9 0.2 fusion.11
  50.1 0.2 fusion.8
  50.2 0.2 fusion.5
  50.4 0.8 %fusion.2 = f32[16,128]{1,0:T(8,128)} fusion(f32[16,128]{1,0:T(8,128)S(1)} %fusion.5, f32[16,128]{1,0:T(8,128)S(1)} %fusion.39, f32[16,138]{1,0:T(8,128)S(1)} %reshape.379), kind=kOutput, calls=%fused_computation.3 | convolution fusion | flops 3470336 | bytes 33408 | tf_op jit(solution)/shard_map/dot_general | solution.py:69
  (35 shorter events, 0.9 us)
Async XLA Ops:
  2.2 7.4 %copy-start = (s32[9]{0:T(128)S(1)}, s32[9]{0:T(128)}, u32[]{:S(2)}) copy-start(s32[9]{0:T(128)} %param.5) | copy-start | bytes 112
  2.2 30.3 %all-to-all-start = ((f32[1,16,128]{2,0,1:T(1,128)}), f32[1,16,128]{2,0,1:T(1,128)S(1)}, u32[]{:S(2)}, u32[]{:S(2)}) async-start(f32[1,16,128]{2,0,1:T(1,128)} %bitcast.4), calls=%async_computation | async-start | bytes 16384 | tf_op jit(solution)/shard_map/all_to_all | solution.py:82
  32.6 12.0 %collective-permute-start.1 = (f32[8,2,128]{2,1,0:T(2,128)S(1)}, f32[8,2,128]{2,1,0:T(2,128)S(1)}, u32[]{:S(2)}, u32[]{:S(2)}) collective-permute-start(f32[8,2,128]{2,1,0:T(2,128)S(1)} %bitcast.106), channel_id=1, source_target_pairs={{1,0},{2,1},{3,2},{4,3},{5,4},{6,5},{7,6},{9,8},{10,9},{11,10},{12... | collective-permute-start | bytes 24584 | tf_op jit(solution)/shard_map/ppermute | solution.py:17
  33.9 10.7 %collective-permute-start = (f32[8,2,128]{2,1,0:T(2,128)S(1)}, f32[8,2,128]{2,1,0:T(2,128)S(1)}, u32[]{:S(2)}, u32[]{:S(2)}) collective-permute-start(f32[8,2,128]{2,1,0:T(2,128)S(1)} %bitcast.107), channel_id=1, source_target_pairs={{0,1},{1,2},{2,3},{3,4},{4,5},{5,6},{6,7},{8,9},{9,10},{10,11},{11... | collective-permute-start | bytes 24584 | tf_op jit(solution)/shard_map/ppermute | solution.py:16
where the time goes:
time: 51.9 us; the launch traced here: 51.2 us
  between operations  29.4 us (57%)
  starting transfers between devices  13.3 us (26%)
  matrix products  4.8 us (9%)
  other arithmetic  2.68 us (5%)
  local copies, waits for them, and re-layouts  1.05 us (2%)
    all_to_all x1, starting transfers between devices, body(): lax.all_to_all(balanced, 'dev', split_axis=1, concat_axis=0, tiled=True)  7.41 us
    ppermute x1, starting transfers between devices, extended_2(): before = lax.ppermute(last, axis, up)  4.55 us
    dot_general x9, matrix products, semblance_scan(): jnp.dot(energy_rows.reshape(shot_count * inner, extended), time_band, pre...  2.05 us
    dot_general x1, matrix products, gain_control(): jnp.einsum('srt,stu->sru', traces * traces, window_mask, precision=lax.Pr...  1.54 us
    ppermute x1, starting transfers between devices, extended_2(): after = lax.ppermute(initial, axis, down)  1.29 us
    mul x4, other arithmetic, semblance_scan(): squared = stacked * stacked  1.22 us
    dot_general x9, matrix products, semblance_scan(): jnp.dot(squared_rows.reshape(shot_count * inner, extended), time_band, pr...  1.21 us
  transfers between devices with their start and end apart: 3, of which 0 were waited for; matrix products, arithmetic and copies ran while one was open for 1% of the time, Pallas kernels for 0%

commit v1 on v0

--- a/solution.py
+++ b/solution.py
@@ -79,7 +79,10 @@
 
 def body(traces, half_window, dip_slopes):
     balanced = gain_control(traces, half_window)
-    gathered = lax.all_to_all(balanced, "dev", split_axis=1, concat_axis=0, tiled=True)
+    gathered = jnp.concatenate(
+        lax.all_to_all(jnp.stack(jnp.split(balanced, lax.axis_size("dev"), axis=1)), "dev", 0, 0),
+        axis=0,
+    )
     widened = extended_2(gathered, (("dev", 1),), 2)
     return semblance_scan(widened, dip_slopes)
 

time: 51.9 us -> 55.8 us (1.075)
  local copies, waits for them, and re-layouts: 1.05 us -> 5.57 us
  matrix products: 4.8 us -> 4.18 us
    unnamed x2 -> x9, local copies, waits for them, and re-layouts: 0.01 us -> 3.96 us
    dot_general x1, matrix products: 1.54 us -> 0.92 us  [gain_control(): jnp.einsum('srt,stu->sru', traces * traces, window_mask, precision=lax.Pr...]
    another operation x0 -> x1, local copies, waits for them, and re-layouts: none -> 0.56 us  [body(): jnp.stack(jnp.split(balanced, lax.axis_size('dev'), axis=1))]
where the time goes in v1:
time: 55.8 us; the launch traced here: 55.1 us
  between operations  29.4 us (53%)
  starting transfers between devices  13.3 us (24%)
  local copies, waits for them, and re-layouts  5.57 us (10%)
  matrix products  4.18 us (7%)
  other arithmetic  2.68 us (5%)
    all_to_all x1, starting transfers between devices, body(): lax.all_to_all(jnp.stack(jnp.split(balanced, lax.axis_size('dev'), axis=1...  7.41 us
    ppermute x1, starting transfers between devices, extended_2(): before = lax.ppermute(last, axis, up)  4.55 us
    unnamed x9, local copies, waits for them, and re-layouts  3.96 us
    dot_general x9, matrix products, semblance_scan(): jnp.dot(energy_rows.reshape(shot_count * inner, extended), time_band, pre...  2.05 us
    ppermute x1, starting transfers between devices, extended_2(): after = lax.ppermute(initial, axis, down)  1.29 us
    mul x4, other arithmetic, semblance_scan(): squared = stacked * stacked  1.22 us
    dot_general x9, matrix products, semblance_scan(): jnp.dot(squared_rows.reshape(shot_count * inner, extended), time_band, pr...  1.21 us
  transfers between devices with their start and end apart: 3, of which 0 were waited for; matrix products, arithmetic and copies ran while one was open for 1% of the time, Pallas kernels for 0%

profile of v1, /device:TPU:0, one launch (start us, length us, event | category | flops | bytes accessed | tf_op | source)
XLA Modules:
  0.0 55.1 jit_solution(9277628737639971283)
XLA Ops:
  0.7 0.9 %fusion.29 = f32[1,16,128]{2,1,0:T(8,128)S(1)} fusion(f32[1,16,128]{2,1,0:T(8,128)} %param.3, s32[]{:T(128)} %bitcast.135, f32[128]{0:T(128)S(1)} %convert_reduce_fusion), kind=kOutput, calls=%fused_computation.39 | convolution fusion | flops 3203072 | bytes 16900 | tf_op jit(solution)/shard_map/srt,stu->sru/dot_general | solution.py:27
  1.6 0.6 %constant_dynamic-update-slice_fusion.7 = f32[8,1,2,128]{3,2,1,0:T(2,128)} fusion(f32[1,16,128]{2,1,0:T(8,128)S(1)} %fusion.29), kind=kLoop, calls=%fused_computation.92 | loop fusion | bytes 2048
  2.2 0.6 %constant_dynamic-update-slice_fusion.6 = f32[8,1,2,128]{3,2,1,0:T(2,128)} fusion(f32[8,1,2,128]{3,2,1,0:T(2,128)} %constant_dynamic-update-slice_fusion.7, f32[1,16,128]{2,1,0:T(8,128)S(1)} %fusion.29), kind=kLoop, calls=%fused_computation.91 | loop fusion | bytes 2048
  2.8 0.6 %constant_dynamic-update-slice_fusion.5 = f32[8,1,2,128]{3,2,1,0:T(2,128)} fusion(f32[8,1,2,128]{3,2,1,0:T(2,128)} %constant_dynamic-update-slice_fusion.6, f32[1,16,128]{2,1,0:T(8,128)S(1)} %fusion.29), kind=kLoop, calls=%fused_computation.90 | loop fusion | bytes 2048
  3.3 0.6 %constant_dynamic-update-slice_fusion.4 = f32[8,1,2,128]{3,2,1,0:T(2,128)} fusion(f32[8,1,2,128]{3,2,1,0:T(2,128)} %constant_dynamic-update-slice_fusion.5, f32[1,16,128]{2,1,0:T(8,128)S(1)} %fusion.29), kind=kLoop, calls=%fused_computation.89 | loop fusion | bytes 2048
  3.9 0.6 %constant_dynamic-update-slice_fusion.3 = f32[8,1,2,128]{3,2,1,0:T(2,128)} fusion(f32[8,1,2,128]{3,2,1,0:T(2,128)} %constant_dynamic-update-slice_fusion.4, f32[1,16,128]{2,1,0:T(8,128)S(1)} %fusion.29), kind=kLoop, calls=%fused_computation.88 | loop fusion | bytes 2048
  4.5 0.6 %constant_dynamic-update-slice_fusion.2 = f32[8,1,2,128]{3,2,1,0:T(2,128)} fusion(f32[8,1,2,128]{3,2,1,0:T(2,128)} %constant_dynamic-update-slice_fusion.3, f32[1,16,128]{2,1,0:T(8,128)S(1)} %fusion.29), kind=kLoop, calls=%fused_computation.87 | loop fusion | bytes 2048
  5.0 0.6 %constant_dynamic-update-slice_fusion.1 = f32[8,1,2,128]{3,2,1,0:T(2,128)} fusion(f32[8,1,2,128]{3,2,1,0:T(2,128)} %constant_dynamic-update-slice_fusion.2, f32[1,16,128]{2,1,0:T(8,128)S(1)} %fusion.29), kind=kLoop, calls=%fused_computation.86 | loop fusion | bytes 2048
  5.6 0.6 %constant_dynamic-update-slice_fusion = f32[8,1,2,128]{3,2,1,0:T(2,128)} fusion(f32[8,1,2,128]{3,2,1,0:T(2,128)} %constant_dynamic-update-slice_fusion.1, f32[1,16,128]{2,1,0:T(8,128)S(1)} %fusion.29), kind=kLoop, calls=%fused_computation.85 | loop fusion | bytes 2048 | tf_op jit(solution)/shard_map/stack | solution.py:83
  6.2 7.4 %all-to-all-start = ((f32[8,1,2,128]{3,2,1,0:T(2,128)}), f32[8,1,2,128]{3,2,1,0:T(2,128)S(1)}, u32[]{:S(2)}, u32[]{:S(2)}) async-start(f32[8,1,2,128]{3,2,1,0:T(2,128)} %constant_dynamic-update-slice_fusion), calls=%async_computation | async-start | bytes 16384 | tf_op jit(solution)/shard_map/all_to_all | solution.py:83
  13.6 0.7 %fusion.105 = (s32[1]{0:T(128)}, s32[1]{0:T(128)}, s32[1]{0:T(128)}, s32[1]{0:T(128)}, s32[1]{0:T(128)}, /*index=5*/s32[1]{0:T(128)}, s32[1]{0:T(128)}, s32[1]{0:T(128)}, s32[1]{0:T(128)}) fusion(s32[9]{0:T(128)S(1)} %copy-done), kind=kLoop, calls=%fused_computation.212 | loop fusion | bytes 72 | tf_op jit(solution)/shard_map/slice | solution.py:47
  36.5 1.3 %collective-permute-start.1 = (f32[8,2,128]{2,1,0:T(2,128)S(1)}, f32[8,2,128]{2,1,0:T(2,128)S(1)}, u32[]{:S(2)}, u32[]{:S(2)}) collective-permute-start(f32[8,2,128]{2,1,0:T(2,128)S(1)} %bitcast.137), channel_id=1, source_target_pairs={{1,0},{2,1},{3,2},{4,3},{5,4},{6,5},{7,6},{9,8},{10,9},{11,10},{12... | collective-permute-start | bytes 24584 | tf_op jit(solution)/shard_map/ppermute | solution.py:17
  37.8 4.5 %collective-permute-start = (f32[8,2,128]{2,1,0:T(2,128)S(1)}, f32[8,2,128]{2,1,0:T(2,128)S(1)}, u32[]{:S(2)}, u32[]{:S(2)}) collective-permute-start(f32[8,2,128]{2,1,0:T(2,128)S(1)} %bitcast.138), channel_id=1, source_target_pairs={{0,1},{1,2},{2,3},{3,4},{4,5},{5,6},{6,7},{8,9},{9,10},{10,11},{11... | collective-permute-start | bytes 24584 | tf_op jit(solution)/shard_map/ppermute | solution.py:16
  48.7 0.3 add_multiply_fusion.6
  49.2 0.3 multiply_add_fusion
  49.9 0.1 fusion.57
  50.1 0.3 add_multiply_fusion
  50.5 0.3 add_multiply_fusion.3
  50.8 0.1 fusion.54
  51.2 0.1 fusion.51
  51.3 0.3 multiply_add_fusion.1
  52.0 0.2 add_multiply_fusion.1
  52.6 0.1 fusion.42
  52.9 0.1 fusion.25
  53.1 0.2 fusion.23
  53.3 0.2 fusion.20
  53.5 0.2 fusion.17
  53.6 0.2 fusion.14
  53.8 0.2 fusion.11
  54.0 0.2 fusion.8
  54.2 0.2 fusion.5
  54.3 0.8 %fusion.2 = f32[16,128]{1,0:T(8,128)} fusion(f32[16,128]{1,0:T(8,128)S(1)} %fusion.5, f32[16,128]{1,0:T(8,128)S(1)} %fusion.39, f32[16,138]{1,0:T(8,128)S(1)} %reshape.380), kind=kOutput, calls=%fused_computation.3 | convolution fusion | flops 3470336 | bytes 33408 | tf_op jit(solution)/shard_map/dot_general | solution.py:69
  (43 shorter events, 1.8 us)
Async XLA Ops:
  6.1 7.4 %copy-start = (s32[9]{0:T(128)S(1)}, s32[9]{0:T(128)}, u32[]{:S(2)}) copy-start(s32[9]{0:T(128)} %param.5) | copy-start | bytes 112
  6.2 30.3 %all-to-all-start = ((f32[8,1,2,128]{3,2,1,0:T(2,128)}), f32[8,1,2,128]{3,2,1,0:T(2,128)S(1)}, u32[]{:S(2)}, u32[]{:S(2)}) async-start(f32[8,1,2,128]{3,2,1,0:T(2,128)} %constant_dynamic-update-slice_fusion), calls=%async_computation | async-start | bytes 16384 | tf_op jit(solution)/shard_map/all_to_all | solution.py:83
  36.5 12.0 %collective-permute-start.1 = (f32[8,2,128]{2,1,0:T(2,128)S(1)}, f32[8,2,128]{2,1,0:T(2,128)S(1)}, u32[]{:S(2)}, u32[]{:S(2)}) collective-permute-start(f32[8,2,128]{2,1,0:T(2,128)S(1)} %bitcast.137), channel_id=1, source_target_pairs={{1,0},{2,1},{3,2},{4,3},{5,4},{6,5},{7,6},{9,8},{10,9},{11,10},{12... | collective-permute-start | bytes 24584 | tf_op jit(solution)/shard_map/ppermute | solution.py:17
  37.8 10.7 %collective-permute-start = (f32[8,2,128]{2,1,0:T(2,128)S(1)}, f32[8,2,128]{2,1,0:T(2,128)S(1)}, u32[]{:S(2)}, u32[]{:S(2)}) collective-permute-start(f32[8,2,128]{2,1,0:T(2,128)S(1)} %bitcast.138), channel_id=1, source_target_pairs={{0,1},{1,2},{2,3},{3,4},{4,5},{5,6},{6,7},{8,9},{9,10},{10,11},{11... | collective-permute-start | bytes 24584 | tf_op jit(solution)/shard_map/ppermute | solution.py:16
